TPU v7x, 32 devices: a whole 2x2x4 slice. The times are simulated.
32 devices in a mesh: clip: 4 (over z), vid: 4 (over y, core), aud: 2 (over x).
Axes of the slice: x: 2, y: 2, z: 4, core: 2. Of those that a mesh axis runs over, the one named last changes fastest.
Arguments:
- video_tokens: bfloat16 [4, 512, 2048], P('clip', 'vid'), may hold values from -6 to 6
- audio_tokens: bfloat16 [4, 512, 2048], P('clip', 'vid'), may hold values from -6 to 6
- qkv_video: bfloat16 [2048, 16, 384], P(None, 'aud'), may hold values from -0.125 to 0.125
- out_video: bfloat16 [16, 128, 2048], P('aud'), may hold values from -0.125 to 0.125
- qkv_audio: bfloat16 [2048, 16, 384], P(None, 'aud'), may hold values from -0.125 to 0.125
- out_audio: bfloat16 [16, 128, 2048], P('aud'), may hold values from -0.125 to 0.125
- gain_video: float32 [2048], replicated, may hold values from 0.5 to 1.5
- gain_audio: float32 [2048], replicated, may hold values from 0.5 to 1.5
- time_from: float32 [65, 2048], replicated, may hold values from -1.8 to 1.8
- time_to: float32 [65, 2048], replicated, may hold values from -1.8 to 1.8
- time_steps: int32 [4, 2], P('clip'), may hold values from 0 to 64, as said below
- windows: int32 [4, 2], P('clip'), may hold values from 32 to 128
- intersection: int32 [4, 16, 2], P('clip'), may hold values from 0 to 16, as said below
Outputs:
- d_video: bfloat16 [4, 512, 2048], P('clip', 'vid')
- d_audio: bfloat16 [4, 512, 2048], P('clip', 'vid')
- grad_qkv_video: float32 [2048, 16, 384], P(('clip', 'vid'), 'aud')
- grad_out_video: float32 [16, 128, 2048], P('aud', None, ('clip', 'vid'))
- grad_qkv_audio: float32 [2048, 16, 384], P(('clip', 'vid'), 'aud')
- grad_out_audio: float32 [16, 128, 2048], P('aud', None, ('clip', 'vid'))
Inputs may be any that keep to these rules, and one draw needn't show every extreme that they name: `time_steps`: column 1 (m) is 1 or more and 2 * m <= column 0 (t) <= 64. `intersection`: entry b holds (lo, hi) with lo < hi, max(b * 32 - 128, 0) <= lo * 32 <= b * 32 and (hi - lo) * 32 <= 160.
All inputs are finite; a program needn't handle non-finite values.
Results may differ from a plain program's by a relative error of at most 0.029.
Values may be sent and summed in bfloat16 or wider, within the bound.
No kernel may reach another device: no remote copies, remote signals or barrier semaphores. Data moves between devices by JAX's collectives and lax.ppermute only.
A program may use at most 128 MiB of HBM per device.

v0:
```python
import jax
import jax.numpy as jnp
from jax import lax
from jax.sharding import PartitionSpec as P

BLK = 32
TGRID = 64
STEPS = 2


EPSILON = 1e-06
PRECISE = lax.Precision.HIGHEST


def padded(block, sides, width):
    for axis, dim in sides:
        count = lax.axis_size(axis)
        forward = [(i, i + 1) for i in range(count - 1)]
        backward = [(target, source) for source, target in forward]
        low = lax.ppermute(
            lax.slice_in_dim(block, block.shape[dim] - width, None, axis=dim), axis, forward
        )
        high = lax.ppermute(lax.slice_in_dim(block, 0, width, axis=dim), axis, backward)
        block = jnp.concatenate([low, block, high], axis=dim)
    return block


def shifted_2(block, axis, distance):
    devices = range(lax.axis_size(axis))
    route = [(i - distance, i) for i in devices if i - distance in devices]
    return lax.ppermute(block, axis, route)


def lookup(time_table, time_index):
    onehot = (jnp.arange(time_table.shape[0], dtype=jnp.int32) == time_index).astype(jnp.float32)
    return jnp.dot(onehot, time_table, precision=PRECISE)


def project_in(current, norm_gain, condition, weight):
    inv_rms = lax.rsqrt(jnp.mean(current * current, -1, keepdims=True) + EPSILON)
    modulation = norm_gain * (1.0 + condition)
    normed = (current * inv_rms * modulation).astype(jnp.bfloat16)
    qkv_rows = jnp.einsum("nd,dhe->nhe", normed, weight, preferred_element_type=jnp.float32).astype(
        jnp.bfloat16
    )
    return (normed, inv_rms, modulation, qkv_rows)


def attend(queries, key_rows, value_rows, key_mask):
    factor = queries.shape[-1] ** (-0.5)
    scores = (
        jnp.einsum("nhe,lhe->hnl", queries, key_rows, preferred_element_type=jnp.float32) * factor
    )
    scores = jnp.where(key_mask[None], scores, -1e30)
    shifted = jnp.exp(scores - jnp.max(scores, -1, keepdims=True))
    attn_prob = shifted / jnp.sum(shifted, -1, keepdims=True)
    rounded = attn_prob.astype(jnp.bfloat16)
    result = jnp.einsum(
        "hnl,lhe->nhe", rounded, value_rows, preferred_element_type=jnp.float32
    ).astype(jnp.bfloat16)
    return (result, attn_prob, rounded)


def attend_back(queries, key_rows, value_rows, attn_prob, rounded, grad_out):
    factor = queries.shape[-1] ** (-0.5)
    grad_prob = jnp.einsum("nhe,lhe->hnl", grad_out, value_rows, preferred_element_type=jnp.float32)
    center = jnp.sum(attn_prob * grad_prob, -1, keepdims=True)
    dscore = (attn_prob * (grad_prob - center) * factor).astype(jnp.bfloat16)
    dquery = jnp.einsum("hnl,lhe->nhe", dscore, key_rows, preferred_element_type=jnp.float32)
    key_grad = jnp.einsum("hnl,nhe->lhe", dscore, queries, preferred_element_type=jnp.float32)
    value_grad = jnp.einsum("hnl,nhe->lhe", rounded, grad_out, preferred_element_type=jnp.float32)
    return (dquery, key_grad, value_grad)


def norm_back(current, inv_rms, modulation, grad_normed):
    scaled = grad_normed * modulation
    return inv_rms * scaled - current * inv_rms**3 * jnp.mean(scaled * current, -1, keepdims=True)


def local(
    video_tokens,
    audio_tokens,
    qkv_video,
    out_video,
    qkv_audio,
    out_audio,
    gain_video,
    gain_audio,
    time_from,
    time_to,
    time_steps,
    windows,
    intersection,
):
    tokens = video_tokens.shape[1]
    head_dim = out_video.shape[1]
    all_tokens = lax.axis_size("vid") * tokens
    offset = lax.axis_index("vid") * tokens
    query_pos = offset + jnp.arange(tokens, dtype=jnp.int32)
    key_pos = offset - tokens + jnp.arange(3 * tokens, dtype=jnp.int32)
    inside = (key_pos >= 0) & (key_pos < all_tokens)
    distance = jnp.abs(query_pos[:, None] - key_pos[None, :])
    query_blk = query_pos // BLK
    key_blk = jnp.clip(key_pos, 0, all_tokens - 1) // BLK
    low_block = intersection[0, :, 0]
    high_block = intersection[0, :, 1]
    video_cross = (
        inside[None, :]
        & (key_blk[None, :] >= low_block[query_blk][:, None])
        & (key_blk[None, :] < high_block[query_blk][:, None])
    )
    audio_cross = (
        inside[None, :]
        & (query_blk[:, None] >= low_block[key_blk][None, :])
        & (query_blk[:, None] < high_block[key_blk][None, :])
    )
    mask_video = jnp.concatenate([inside[None, :] & (distance < windows[0, 0]), video_cross], 1)
    mask_audio = jnp.concatenate([audio_cross, inside[None, :] & (distance < windows[0, 1])], 1)

    def network(video_now, audio_now, condition):
        video_norm, video_inv, video_mod, video_rows = project_in(
            video_now, gain_video, condition, qkv_video
        )
        audio_norm, audio_inv, audio_mod, audio_rows = project_in(
            audio_now, gain_audio, condition, qkv_audio
        )
        stacked = jnp.stack(
            [
                video_rows[:, :, head_dim:].reshape(tokens, -1),
                audio_rows[:, :, head_dim:].reshape(tokens, -1),
            ]
        )
        widened = padded(stacked, (("vid", 1),), tokens)
        widened = widened.reshape(2, widened.shape[1], -1, 2 * head_dim)
        key_rows = jnp.concatenate([widened[0, :, :, :head_dim], widened[1, :, :, :head_dim]], 0)
        value_rows = jnp.concatenate([widened[0, :, :, head_dim:], widened[1, :, :, head_dim:]], 0)
        video_out, video_prob, video_round = attend(
            video_rows[:, :, :head_dim], key_rows, value_rows, mask_video
        )
        audio_out, audio_prob, audio_round = attend(
            audio_rows[:, :, :head_dim], key_rows, value_rows, mask_audio
        )
        video_part = jnp.einsum(
            "nhe,hef->nf", video_out, out_video, preferred_element_type=jnp.float32
        )
        audio_part = jnp.einsum(
            "nhe,hef->nf", audio_out, out_audio, preferred_element_type=jnp.float32
        )
        video_field, audio_field = (
            lax.psum(video_part.astype(jnp.bfloat16), "aud").astype(jnp.float32),
            lax.psum(audio_part.astype(jnp.bfloat16), "aud").astype(jnp.float32),
        )
        saved = (
            video_norm,
            video_inv,
            video_mod,
            video_rows,
            audio_norm,
            audio_inv,
            audio_mod,
            audio_rows,
            key_rows,
            value_rows,
            video_out,
            video_prob,
            video_round,
            audio_out,
            audio_prob,
            audio_round,
        )
        return (video_field, audio_field, saved)

    start_video = video_tokens[0].astype(jnp.float32)
    start_audio = audio_tokens[0].astype(jnp.float32)
    time_now = time_steps[0, 0]
    stride = time_steps[0, 1]
    euler_step = -stride.astype(jnp.float32) / TGRID
    video_now, audio_now = (start_video, start_audio)
    for teacher_step in range(STEPS):
        time_level = time_now - teacher_step * stride
        condition = lookup(time_from, time_level) + lookup(time_to, time_level)
        video_field, audio_field, unused = network(video_now, audio_now, condition)
        video_now = video_now + euler_step * video_field
        audio_now = audio_now + euler_step * audio_field
    condition = lookup(time_from, time_now) + lookup(time_to, time_now - STEPS * stride)
    video_field, audio_field, saved = network(start_video, start_audio, condition)
    (
        video_norm,
        video_inv,
        video_mod,
        video_rows,
        audio_norm,
        audio_inv,
        audio_mod,
        audio_rows,
        key_rows,
        value_rows,
        video_out,
        video_prob,
        video_round,
        audio_out,
        audio_prob,
        audio_round,
    ) = saved
    span_time = -(STEPS * stride).astype(jnp.float32) / TGRID
    video_diff = start_video + span_time * video_field - video_now
    audio_diff = start_audio + span_time * audio_field - audio_now
    video_grad = (span_time * video_diff).astype(jnp.bfloat16)
    audio_grad = (span_time * audio_diff).astype(jnp.bfloat16)
    video_wout = jnp.einsum(
        "nhe,nf->hef", video_out, video_grad, preferred_element_type=jnp.float32
    )
    audio_wout = jnp.einsum(
        "nhe,nf->hef", audio_out, audio_grad, preferred_element_type=jnp.float32
    )
    video_dout = jnp.einsum(
        "nf,hef->nhe", video_grad, out_video, preferred_element_type=jnp.float32
    ).astype(jnp.bfloat16)
    audio_dout = jnp.einsum(
        "nf,hef->nhe", audio_grad, out_audio, preferred_element_type=jnp.float32
    ).astype(jnp.bfloat16)
    video_dq, video_dk, video_dv = attend_back(
        video_rows[:, :, :head_dim], key_rows, value_rows, video_prob, video_round, video_dout
    )
    audio_dq, audio_dk, audio_dv = attend_back(
        audio_rows[:, :, :head_dim], key_rows, value_rows, audio_prob, audio_round, audio_dout
    )
    length = key_rows.shape[0] // 2
    key_grads = jnp.concatenate([video_dk + audio_dk, video_dv + audio_dv], -1).reshape(
        2, length, -1
    )
    from_right = shifted_2(key_grads[:, :tokens].astype(jnp.bfloat16), "vid", -1).astype(
        jnp.float32
    )
    from_left = shifted_2(key_grads[:, 2 * tokens :].astype(jnp.bfloat16), "vid", 1).astype(
        jnp.float32
    )
    owned = key_grads[:, tokens : 2 * tokens] + from_right + from_left
    owned = owned.reshape(2, tokens, -1, 2 * head_dim)
    video_dqkv = jnp.concatenate([video_dq, owned[0]], -1).astype(jnp.bfloat16)
    audio_dqkv = jnp.concatenate([audio_dq, owned[1]], -1).astype(jnp.bfloat16)
    video_wqkv = jnp.einsum(
        "nd,nhe->dhe", video_norm, video_dqkv, preferred_element_type=jnp.float32
    )
    audio_wqkv = jnp.einsum(
        "nd,nhe->dhe", audio_norm, audio_dqkv, preferred_element_type=jnp.float32
    )
    video_part = jnp.einsum(
        "nhe,dhe->nd", video_dqkv, qkv_video, preferred_element_type=jnp.float32
    )
    audio_part = jnp.einsum(
        "nhe,dhe->nd", audio_dqkv, qkv_audio, preferred_element_type=jnp.float32
    )
    video_back, audio_back = (
        lax.psum(video_part.astype(jnp.bfloat16), "aud").astype(jnp.float32),
        lax.psum(audio_part.astype(jnp.bfloat16), "aud").astype(jnp.float32),
    )
    d_video = (video_diff + norm_back(start_video, video_inv, video_mod, video_back)).astype(
        jnp.bfloat16
    )
    d_audio = (audio_diff + norm_back(start_audio, audio_inv, audio_mod, audio_back)).astype(
        jnp.bfloat16
    )
    summed = (
        lax.psum_scatter(
            video_wqkv.astype(jnp.bfloat16), ("clip", "vid"), scatter_dimension=0, tiled=True
        ).astype(jnp.float32),
        lax.psum_scatter(
            video_wout.astype(jnp.bfloat16), ("clip", "vid"), scatter_dimension=2, tiled=True
        ).astype(jnp.float32),
        lax.psum_scatter(
            audio_wqkv.astype(jnp.bfloat16), ("clip", "vid"), scatter_dimension=0, tiled=True
        ).astype(jnp.float32),
        lax.psum_scatter(
            audio_wout.astype(jnp.bfloat16), ("clip", "vid"), scatter_dimension=2, tiled=True
        ).astype(jnp.float32),
    )
    return (d_video[None], d_audio[None], summed[0], summed[1], summed[2], summed[3])


def solution(mesh):
    return jax.shard_map(
        local,
        mesh=mesh,
        in_specs=(
            P("clip", "vid", None),
            P("clip", "vid", None),
            P(None, "aud", None),
            P("aud", None, None),
            P(None, "aud", None),
            P("aud", None, None),
            P(),
            P(),
            P(),
            P(),
            P("clip", None),
            P("clip", None),
            P("clip", None, None),
        ),
        out_specs=(
            P("clip", "vid", None),
            P("clip", "vid", None),
            P(("clip", "vid"), "aud", None),
            P("aud", None, ("clip", "vid")),
            P(("clip", "vid"), "aud", None),
            P("aud", None, ("clip", "vid")),
        ),
        check_vma=False,
    )
```

profile of v0, /device:TPU:0, one launch (start us, length us, event | category | flops | bytes accessed | tf_op | source)
XLA Modules:
  0.0 931.6 jit_solution(10172662448578137054)
XLA Ops:
  18.8 7.4 fusion.105
  27.5 7.3 fusion.96
  42.8 7.3 fusion.99
  51.4 7.3 fusion.108
  68.9 10.1 %bitcast_select_fusion.17 = s32[128]{0:T(128)S(1)} fusion(s32[]{:T(128)} %bitcast.36, s32[]{:T(128)} %bitcast.37, s32[]{:T(128)} %bitcast.38, s32[]{:T(128)} %bitcast.39, s32[]{:T(128)} %bitcast.40, s32[]{:T(128)} %bitcast.42, s32[]{:T(128)} %bitcast.41, s32[]{:T(128)} %bitcast.19, s32[]{:T(128)} %bitcast.21, s32[]{:T(128)} %bitcast.23, s32[]{:T(128)} %bitcast.25, ...), kind=kLoop, calls=%fused_computation.322 | loop fusion | flops 6272 | bytes 580 | tf_op jit(solution)/shard_map/gather | solution.py:109
  79.0 9.8 %bitcast_select_fusion.16 = s32[128]{0:T(128)S(1)} fusion(s32[]{:T(128)} %bitcast.53, s32[]{:T(128)} %bitcast.54, s32[]{:T(128)} %bitcast.55, s32[]{:T(128)} %bitcast.56, s32[]{:T(128)} %bitcast.57, s32[]{:T(128)} %bitcast.59, s32[]{:T(128)} %bitcast.58, s32[]{:T(128)} %bitcast.44, s32[]{:T(128)} %bitcast.45, s32[]{:T(128)} %bitcast.46, s32[]{:T(128)} %bitcast.47, ...), kind=kLoop, calls=%fused_computation.321 | loop fusion | flops 6272 | bytes 580 | tf_op jit(solution)/shard_map/gather | solution.py:110
  163.5 34.6 %all-reduce.11.cloned.1.call-done = (bf16[128,2048]{1,0:T(8,128)(2,1)}, bf16[128,2048]{1,0:T(8,128)(2,1)}) async-done(((bf16[128,2048]{1,0:T(8,128)(2,1)}, bf16[128,2048]{1,0:T(8,128)(2,1)}), (bf16[128,2048]{1,0:T(8,128)(2,1)}, bf16[128,2048]{1,0:T(8,128)(2,1)})) %all-reduce.11.cloned.1.call-update) | async-done | bytes 1048592 | tf_op jit(solution)/shard_map/psum | solution.py:151
  200.8 7.6 fusion.102
  209.4 7.3 fusion.111
  260.7 69.1 %all-reduce.9.cloned.1.call-done = (bf16[128,2048]{1,0:T(8,128)(2,1)}, bf16[128,2048]{1,0:T(8,128)(2,1)}, bf16[128,2048]{1,0:T(8,128)(2,1)}, bf16[128,2048]{1,0:T(8,128)(2,1)}) async-done(((bf16[128,2048]{1,0:T(8,128)(2,1)}, bf16[128,2048]{1,0:T(8,128)(2,1)}, bf16[128,2048]{1,0:T(8,128)(2,1)}, bf16[128,2048]{1,0:T(8,128)(2,1)}), (bf16[128,2048]{1,0:T(8,128)(2,1)}, bf16[128,2048]{1,0:T(8,128)(2,1)}, ...) | async-done | bytes 2097168 | tf_op jit(solution)/shard_map/psum | solution.py:150
  344.0 12.0 %fusion.57 = f32[8,128,768]{2,1,0:T(8,128)} fusion(f32[8,128,768]{2,1,0:T(8,128)} %fusion.292, bf16[128,8,384]{2,0,1:T(8,128)(2,1)} %copy-done.40, f32[8,128,768]{2,1,0:T(8,128)} %get-tuple-element.109, f32[8,128]{1,0:T(8,128)S(1)} %get-tuple-element.108), kind=kOutput, calls=%fused_computation.95 | convolution fusion | flops 206833408 | bytes 15998976 | tf_op jit(solution)/shard_map/hnl,nhe->lhe/dot_general | solution.py:70
  361.2 13.0 %add_bitcast_fusion.1 = f32[768,8,128]{0,2,1:T(8,128)} fusion(f32[8,128,768]{2,1,0:T(8,128)} %fusion.57, f32[8,128,768]{2,1,0:T(8,128)} %fusion.291, bf16[128,8,384]{2,0,1:T(8,128)(2,1)} %copy-done.39, f32[8,128,768]{2,1,0:T(8,128)} %get-tuple-element.113, f32[8,128]{1,0:T(8,128)S(1)} %get-tuple-element.112), kind=kOutput, calls=%fused_computation.35 | convolution fusion | flops 207619840 | bytes 19144704 | tf_op jit(solution)/shard_map/hnl,nhe->lhe/dot_general | solution.py:70
  380.2 8.2 reshape.270
  402.2 11.5 %fusion.137 = bf16[128,8,128]{0,2,1:T(8,128)(2,1)S(1)} fusion(f32[8,128,768]{2,1,0:T(8,128)} %fusion.291, bf16[384,8,128]{2,0,1:T(8,128)(2,1)} %bitcast.344, bf16[384,8,128]{2,0,1:T(8,128)(2,1)S(1)} %bitcast.340, f32[8,128,768]{2,1,0:T(8,128)} %get-tuple-element.113, f32[8,128]{1,0:T(8,128)S(1)} %get-tuple-element.112), kind=kOutput, calls=%fused_computation.160 | convolution fusion | flops 210110208 | bytes 8130560 | tf_op jit(solution)/shard_map/hnl,lhe->nhe/dot_general | solution.py:69
  414.6 11.5 %fusion.134 = bf16[128,8,128]{0,2,1:T(8,128)(2,1)S(1)} fusion(f32[8,128,768]{2,1,0:T(8,128)} %fusion.292, bf16[384,8,128]{2,0,1:T(8,128)(2,1)} %bitcast.345, bf16[384,8,128]{2,0,1:T(8,128)(2,1)S(1)} %bitcast.341, f32[8,128,768]{2,1,0:T(8,128)} %get-tuple-element.109, f32[8,128]{1,0:T(8,128)S(1)} %get-tuple-element.108), kind=kOutput, calls=%fused_computation.159 | convolution fusion | flops 210110208 | bytes 8130560 | tf_op jit(solution)/shard_map/hnl,lhe->nhe/dot_general | solution.py:69
  433.2 9.8 %fusion.45 = bf16[128,2048]{1,0:T(8,128)(2,1)} fusion(bf16[2048,8,384]{2,1,0:T(8,128)(2,1)} %param.15, bf16[128,8,256]{2,0,1:T(8,128)(2,1)S(1)} %copy.117, bf16[128,8,128]{2,0,1:T(8,128)(2,1)S(1)} %copy.116), kind=kOutput, calls=%fused_computation.73 | convolution fusion | flops 1612447744 | bytes 13893632 | tf_op jit(solution)/shard_map/nhe,dhe->nd/dot_general | solution.py:248
  443.0 9.9 %fusion.42 = bf16[128,2048]{1,0:T(8,128)(2,1)} fusion(bf16[2048,8,384]{2,1,0:T(8,128)(2,1)} %param.17, bf16[128,8,256]{2,0,1:T(8,128)(2,1)S(1)} %copy-done.30, bf16[128,8,128]{2,0,1:T(8,128)(2,1)S(1)} %copy-done.35), kind=kOutput, calls=%fused_computation.72 | convolution fusion | flops 1612447744 | bytes 13893632 | tf_op jit(solution)/shard_map/nhe,dhe->nd/dot_general | solution.py:251
  457.1 6.8 copy.147
  474.4 6.9 copy.145
  487.6 7.5 convolution_convert_fusion
  509.5 60.4 %reduce-scatter.15.cloned.1.call-done = bf16[128,1024]{1,0:T(8,128)(2,1)} async-done(((bf16[2048,1024]{1,0:T(8,128)(2,1)}), bf16[128,1024]{1,0:T(8,128)(2,1)}) %reduce-scatter.15.cloned.1.call-update) | async-done | bytes 262160
  572.0 73.0 %reduce-scatter.13.cloned.1.call-done = bf16[128,1024]{1,0:T(8,128)(2,1)} async-done(((bf16[2048,1024]{1,0:T(8,128)(2,1)}), bf16[128,1024]{1,0:T(8,128)(2,1)}) %reduce-scatter.13.cloned.1.call-update) | async-done | bytes 262160
  647.2 136.0 %reduce-scatter.11.cloned.1.call-done = bf16[128,8,384]{2,0,1:T(8,128)(2,1)} async-done(((bf16[2048,8,384]{2,0,1:T(8,128)(2,1)}), bf16[128,8,384]{2,0,1:T(8,128)(2,1)}) %reduce-scatter.11.cloned.1.call-update) | async-done | bytes 786448 | tf_op jit(solution)/shard_map/reduce_scatter | solution.py:271
  785.9 135.8 %reduce-scatter.9.cloned.1.call-done = bf16[128,8,384]{2,0,1:T(8,128)(2,1)} async-done(((bf16[2048,8,384]{2,0,1:T(8,128)(2,1)}), bf16[128,8,384]{2,0,1:T(8,128)(2,1)}) %reduce-scatter.9.cloned.1.call-update) | async-done | bytes 786448 | tf_op jit(solution)/shard_map/reduce_scatter | solution.py:265
  (281 shorter events, 242.7 us)
Async XLA Ops:
  7.2 190.9 %all-reduce.11.cloned.1.call-start = ((), (), s32[]{:S(2)}) async-start(), calls=%async_computation.10 | async-start | bytes 2097152 | tf_op jit(solution)/shard_map/psum | solution.py:151
  16.6 34.8 %copy-start.54 = (f32[128]{0:T(128)}, f32[128]{0:T(128)S(1)}, u32[]{:S(2)}) copy-start(f32[128]{0:T(128)S(1)} %get-tuple-element.93) | copy-start | bytes 1540
  17.2 25.6 %copy-start.56 = (f32[128]{0:T(128)}, f32[128]{0:T(128)S(1)}, u32[]{:S(2)}) copy-start(f32[128]{0:T(128)S(1)} %get-tuple-element.95) | copy-start | bytes 1540
  36.0 14.1 %copy-start.21 = (bf16[128,8,256]{0,2,1:T(8,128)(2,1)}, bf16[128,8,256]{0,2,1:T(8,128)(2,1)S(1)}, u32[]{:S(2)}) copy-start(bf16[128,8,256]{0,2,1:T(8,128)(2,1)S(1)} %copy.84) | copy-start | bytes 1572868
  37.2 88.3 %collective-permute-start.1 = (bf16[2,128,2048]{1,2,0:T(8,128)(2,1)}, bf16[2,128,2048]{1,2,0:T(8,128)(2,1)}, u32[]{:S(2)}, u32[]{:S(2)}) collective-permute-start(bf16[2,128,2048]{1,2,0:T(8,128)(2,1)} %pad_maximum_fusion.10), channel_id=1, source_target_pairs={{2,0},{4,2},{6,4},{3,1},{5,3},{7,5},{10,8},{12,10},{14,12},{11,9},... | collective-permute-start | bytes 3145736 | tf_op jit(solution)/shard_map/ppermute | solution.py:23
  38.5 87.0 %collective-permute-start = (bf16[2,128,2048]{1,2,0:T(8,128)(2,1)}, bf16[2,128,2048]{1,2,0:T(8,128)(2,1)}, u32[]{:S(2)}, u32[]{:S(2)}) collective-permute-start(bf16[2,128,2048]{1,2,0:T(8,128)(2,1)} %pad_maximum_fusion.10), channel_id=1, source_target_pairs={{0,2},{2,4},{4,6},{1,3},{3,5},{5,7},{8,10},{10,12},{12,14},{9,11},... | collective-permute-start | bytes 3145736 | tf_op jit(solution)/shard_map/ppermute | solution.py:20
  59.6 39.0 %copy-start.58 = (s32[1,2]{1,0:T(1,128)S(1)}, s32[1,2]{1,0:T(1,128)}, u32[]{:S(2)}) copy-start(s32[1,2]{1,0:T(1,128)} %param.24) | copy-start | bytes 28
  61.0 52.3 %collective-permute-start.3 = (bf16[2,128,2048]{1,2,0:T(8,128)(2,1)}, bf16[2,128,2048]{1,2,0:T(8,128)(2,1)}, u32[]{:S(2)}, u32[]{:S(2)}) collective-permute-start(bf16[2,128,2048]{1,2,0:T(8,128)(2,1)} %pad_maximum_fusion.11), channel_id=1, source_target_pairs={{2,0},{4,2},{6,4},{3,1},{5,3},{7,5},{10,8},{12,10},{14,12},{11,9},... | collective-permute-start | bytes 3145736 | tf_op jit(solution)/shard_map/ppermute | solution.py:23
  62.2 51.1 %collective-permute-start.2 = (bf16[2,128,2048]{1,2,0:T(8,128)(2,1)}, bf16[2,128,2048]{1,2,0:T(8,128)(2,1)}, u32[]{:S(2)}, u32[]{:S(2)}) collective-permute-start(bf16[2,128,2048]{1,2,0:T(8,128)(2,1)} %pad_maximum_fusion.11), channel_id=1, source_target_pairs={{0,2},{2,4},{4,6},{1,3},{3,5},{5,7},{8,10},{10,12},{12,14},{9,11},... | collective-permute-start | bytes 3145736 | tf_op jit(solution)/shard_map/ppermute | solution.py:20
  128.8 33.3 %copy-start.13 = (bf16[384,8,128]{0,2,1:T(8,128)(2,1)}, bf16[384,8,128]{0,2,1:T(8,128)(2,1)S(1)}, u32[]{:S(2)}) copy-start(bf16[384,8,128]{0,2,1:T(8,128)(2,1)S(1)} %get-tuple-element.36) | copy-start | bytes 2359300
  129.2 27.2 %copy-start.10 = (bf16[1,384,8,128]{3,1,2,0:T(8,128)(2,1)}, bf16[1,384,8,128]{3,1,2,0:T(8,128)(2,1)S(1)}, u32[]{:S(2)}) copy-start(bf16[1,384,8,128]{3,1,2,0:T(8,128)(2,1)S(1)} %copy.149) | copy-start | bytes 2359300
  131.0 25.4 %copy-start.12 = (bf16[1,384,8,128]{3,1,2,0:T(8,128)(2,1)}, bf16[1,384,8,128]{3,1,2,0:T(8,128)(2,1)S(1)}, u32[]{:S(2)}) copy-start(bf16[1,384,8,128]{3,1,2,0:T(8,128)(2,1)S(1)} %copy.150) | copy-start | bytes 2359300
  156.2 173.6 %all-reduce.9.cloned.1.call-start = ((), (), s32[]{:S(2)}) async-start(), calls=%async_computation.9 | async-start | bytes 4194304 | tf_op jit(solution)/shard_map/psum | solution.py:150
  221.1 12.3 %collective-permute-start.5 = (bf16[2,128,2048]{1,2,0:T(8,128)(2,1)S(1)}, bf16[2,128,2048]{1,2,0:T(8,128)(2,1)S(1)}, u32[]{:S(2)}, u32[]{:S(2)}) collective-permute-start(bf16[2,128,2048]{1,2,0:T(8,128)(2,1)S(1)} %pad_maximum_fusion.12), channel_id=1, source_target_pairs={{2,0},{4,2},{6,4},{3,1},{5,3},{7,5},{10,8},{12,10},{14,12},{11,9},... | collective-permute-start | bytes 3145736 | tf_op jit(solution)/shard_map/ppermute | solution.py:23
  222.5 10.8 %collective-permute-start.4 = (bf16[2,128,2048]{1,2,0:T(8,128)(2,1)S(1)}, bf16[2,128,2048]{1,2,0:T(8,128)(2,1)S(1)}, u32[]{:S(2)}, u32[]{:S(2)}) collective-permute-start(bf16[2,128,2048]{1,2,0:T(8,128)(2,1)S(1)} %pad_maximum_fusion.12), channel_id=1, source_target_pairs={{0,2},{2,4},{4,6},{1,3},{3,5},{5,7},{8,10},{10,12},{12,14},{9,11},... | collective-permute-start | bytes 3145736 | tf_op jit(solution)/shard_map/ppermute | solution.py:20
  254.7 75.0 %copy-start.9 = (bf16[128,2048]{1,0:T(8,128)(2,1)S(1)}, bf16[128,2048]{1,0:T(8,128)(2,1)}, u32[]{:S(2)}) copy-start(bf16[128,2048]{1,0:T(8,128)(2,1)} %get-tuple-element.31) | copy-start | bytes 1572868
  260.2 242.1 %all-reduce.7.cloned.1.call-start = ((), (), s32[]{:S(2)}) async-start(), calls=%async_computation.8 | async-start | bytes 2097152 | tf_op jit(solution)/shard_map/psum | solution.py:255
  393.5 32.9 %collective-permute-start.6 = (bf16[2,128,2048]{1,2,0:T(8,128)(2,1)}, bf16[2,128,2048]{1,2,0:T(8,128)(2,1)}, u32[]{:S(2)}, u32[]{:S(2)}) collective-permute-start(bf16[2,128,2048]{1,2,0:T(8,128)(2,1)} %get-tuple-element.32), channel_id=1, source_target_pairs={{2,0},{4,2},{6,4},{3,1},{5,3},{7,5},{10,8},{12,10},{14,12},{11,9},... | collective-permute-start | bytes 3145736 | tf_op jit(solution)/shard_map/ppermute | solution.py:31
  394.8 31.6 %collective-permute-start.7 = (bf16[2,128,2048]{1,2,0:T(8,128)(2,1)}, bf16[2,128,2048]{1,2,0:T(8,128)(2,1)}, u32[]{:S(2)}, u32[]{:S(2)}) collective-permute-start(bf16[2,128,2048]{1,2,0:T(8,128)(2,1)} %get-tuple-element.33), channel_id=1, source_target_pairs={{0,2},{2,4},{4,6},{1,3},{3,5},{5,7},{8,10},{10,12},{12,14},{9,11},... | collective-permute-start | bytes 3145736 | tf_op jit(solution)/shard_map/ppermute | solution.py:31
  453.0 117.0 %reduce-scatter.15.cloned.1.call-start = ((), (), s32[]{:S(2)}) async-start(), calls=%async_computation.7 | async-start | bytes 4456448
  469.2 175.8 %reduce-scatter.13.cloned.1.call-start = ((), (), s32[]{:S(2)}) async-start(), calls=%async_computation.6 | async-start | bytes 4456448
  486.6 296.7 %reduce-scatter.11.cloned.1.call-start = ((), (), s32[]{:S(2)}) async-start(), calls=%async_computation.5 | async-start | bytes 13369344 | tf_op jit(solution)/shard_map/reduce_scatter | solution.py:271
  495.1 426.6 %reduce-scatter.9.cloned.1.call-start = ((), (), s32[]{:S(2)}) async-start(), calls=%async_computation.4 | async-start | bytes 13369344 | tf_op jit(solution)/shard_map/reduce_scatter | solution.py:265
  645.0 279.4 %copy-start.1 = (f32[65,2048]{1,0:T(8,128)S(1)}, f32[65,2048]{1,0:T(8,128)}, u32[]{:S(2)}) copy-start(f32[65,2048]{1,0:T(8,128)} %param.22) | copy-start | bytes 1597444
  (55 other events, 259.1 us)
Sparse Core Ops, SparseCore 0:
  156.3 41.7 all-reduce.10
  260.3 69.3 all-reduce.8
  453.1 40.1 all-reduce.6
  497.4 72.4 reduce-scatter.14
  573.7 71.3 reduce-scatter.12
  649.5 133.6 reduce-scatter.10
  787.8 133.8 reduce-scatter.8
where the time goes:
time: 940 us; the launch traced here: 932 us
  waiting for transfers between devices  509 us (54%)
  matrix products  196 us (21%)
  other arithmetic  98.9 us (11%)
  local copies, waits for them, and re-layouts  85.4 us (9%)
  starting transfers between devices  23.6 us (3%)
  between operations  18.6 us (2%)
    reduce_scatter x1, waiting for transfers between devices, local(): lax.psum_scatter(audio_wqkv.astype(jnp.bfloat16), ('clip', 'vid'), scatte...  136 us
    reduce_scatter x1, waiting for transfers between devices, local(): lax.psum_scatter(video_wqkv.astype(jnp.bfloat16), ('clip', 'vid'), scatte...  136 us
    unnamed x9, waiting for transfers between devices  134 us
    psum x1, waiting for transfers between devices, network(): lax.psum(video_part.astype(jnp.bfloat16), 'aud').astype(jnp.float32)  69.1 us
    unnamed x144, local copies, waits for them, and re-layouts  50.5 us
    dot_general x6, matrix products, project_in(): jnp.einsum('nd,dhe->nhe', normed, weight, preferred_element_type=jnp.floa...  44.2 us
    psum x1, waiting for transfers between devices, network(): lax.psum(audio_part.astype(jnp.bfloat16), 'aud').astype(jnp.float32)  34.6 us
    dot_general x2, matrix products, attend_back(): jnp.einsum('hnl,nhe->lhe', dscore, queries, preferred_element_type=jnp.fl...  25 us
  transfers between devices with their start and end apart: 15, of which 6 were waited for; matrix products, arithmetic and copies ran while one was open for 19% of the time, Pallas kernels for 0%

commit v1 on v0

v1 whole, which is shorter than its diff:
```python
import functools

import jax
import jax.numpy as jnp
from jax import lax
from jax.experimental import pallas as pl
from jax.experimental.pallas import tpu as pltpu
from jax.sharding import PartitionSpec as P

BLK = 32
TGRID = 64
STEPS = 2
EPSILON = 1e-06
MASKED = -1e30
F32 = jnp.float32
BF16 = jnp.bfloat16
NT = (((1,), (1,)), ((), ()))
TN = (((0,), (0,)), ((), ()))


def swap(block, axis, bit):
    count = lax.axis_size(axis)
    return lax.ppermute(block, axis, [(i, i ^ (1 << bit)) for i in range(count)])


def shift(block, axis, distance):
    count = lax.axis_size(axis)
    route = [(i, i + distance) for i in range(count) if 0 <= i + distance < count]
    return lax.ppermute(block, axis, route)


def bits_of(count):
    return count.bit_length() - 1


def gather_steps():
    steps = [("clip", 0)] if lax.axis_size("clip") > 1 else []
    return steps + [("vid", bit) for bit in reversed(range(bits_of(lax.axis_size("vid"))))]


def gather_tokens(block):
    gathered = block[None]
    for axis, bit in gather_steps():
        gathered = jnp.concatenate([gathered, swap(gathered, axis, bit)], 0)
    return gathered


def split_columns(block):
    m, n, width = block.shape
    steps = gather_steps()
    devices = lax.axis_size("clip") * lax.axis_size("vid")
    late = devices >> len(steps)
    parts = block.reshape(m, n, devices, width // devices).transpose(2, 0, 1, 3)
    return parts.reshape((late,) + (2,) * len(steps) + parts.shape[1:])


def scatter_columns(block):
    parts = split_columns(block)[None]
    for axis, bit in gather_steps():
        mine = (lax.axis_index(axis) >> bit) & 1
        keep = lax.dynamic_index_in_dim(parts, mine, 2, keepdims=False)
        send = lax.dynamic_index_in_dim(parts, 1 - mine, 2, keepdims=False)
        parts = jnp.concatenate([keep, swap(send, axis, bit)], 0)
    return parts


def reduce_late(partial):
    for bit in reversed(range(1, bits_of(lax.axis_size("clip")))):
        partial = partial.reshape((2, partial.shape[0] // 2) + partial.shape[1:])
        mine = (lax.axis_index("clip") >> bit) & 1
        keep = lax.dynamic_index_in_dim(partial, mine, 0, keepdims=False)
        send = lax.dynamic_index_in_dim(partial, 1 - mine, 0, keepdims=False)
        partial = keep + swap(send.astype(BF16), "clip", bit).astype(F32)
    return partial[0]


def sum_groups(partial):
    count = lax.axis_size("aud")
    total = partial.astype(F32)
    for step in range(1, count):
        total = total + lax.ppermute(
            partial, "aud", [(i, i ^ step) for i in range(count)]
        ).astype(F32)
    return total


def prepare_kernel(
    steps, place, windows, lists, time_from, time_to, gain_v, gain_a, bias, mods, *, tokens
):
    time_now, stride = steps[0], steps[1]
    levels = [(time_now, time_now), (time_now - stride, time_now - stride)]
    levels.append((time_now, time_now - STEPS * stride))
    for row, (start, end) in enumerate(levels):
        condition = time_from[pl.ds(start, 1), :] + time_to[pl.ds(end, 1), :]
        mods[2 * row : 2 * row + 1, :] = gain_v[...] * (1.0 + condition)
        mods[2 * row + 1 : 2 * row + 2, :] = gain_a[...] * (1.0 + condition)

    device = place[0]
    blocks = tokens // BLK
    all_blocks = place[1]
    shape = (tokens, 3 * tokens)
    row_pos = device * tokens + lax.broadcasted_iota(jnp.int32, shape, 0)
    column = lax.broadcasted_iota(jnp.int32, shape, 1)
    column_pos = (device - 1) * tokens + column
    inside = (column_pos >= 0) & (column_pos < all_blocks * BLK)
    distance = jnp.abs(row_pos - column_pos)
    row_blk = device * blocks + lax.broadcasted_iota(jnp.int32, shape, 0) // BLK
    column_blk = (device - 1) * blocks + column // BLK

    def fill(admitted, part, side):
        bias[part, :, side * 3 * tokens : (side + 1) * 3 * tokens] = jnp.where(
            admitted, 0.0, MASKED
        ).astype(F32)

    fill(inside & (distance < windows[0]), 0, 0)
    fill(inside & (distance < windows[1]), 1, 1)
    low = jnp.zeros(shape, jnp.int32)
    high = jnp.zeros(shape, jnp.int32)
    for block in range(blocks):
        here = row_blk == device * blocks + block
        low = jnp.where(here, lists[device * blocks + block, 0], low)
        high = jnp.where(here, lists[device * blocks + block, 1], high)
    fill(inside & (column_blk >= low) & (column_blk < high), 0, 1)
    low = jnp.zeros(shape, jnp.int32)
    high = jnp.zeros(shape, jnp.int32)
    for block in range(3 * blocks):
        index = (device - 1) * blocks + block
        safe = jnp.clip(index, 0, all_blocks - 1)
        here = column_blk == index
        low = jnp.where(here, lists[safe, 0], low)
        high = jnp.where(here, lists[safe, 1], high)
    fill(inside & (row_blk >= low) & (row_blk < high), 1, 0)


def prepare(time_steps, windows, intersection, time_from, time_to, gain_video, gain_audio, tokens):
    place = jnp.stack([lax.axis_index("vid"), lax.axis_size("vid") * tokens // BLK])
    smem = pl.BlockSpec(memory_space=pltpu.SMEM)
    vmem = pl.BlockSpec(memory_space=pltpu.VMEM)
    width = gain_video.shape[0]
    return pl.pallas_call(
        functools.partial(prepare_kernel, tokens=tokens),
        out_shape=(
            jax.ShapeDtypeStruct((2, tokens, 6 * tokens), F32),
            jax.ShapeDtypeStruct((6, width), F32),
        ),
        in_specs=[smem] * 4 + [vmem] * 4,
        out_specs=(vmem, vmem),
        name="prepare",
    )(
        time_steps[0],
        place.astype(jnp.int32),
        windows[0],
        intersection[0],
        time_from,
        time_to,
        gain_video[None],
        gain_audio[None],
    )


def soft(queries, keys, bias, factor):
    scores = lax.dot_general(queries, keys, NT, preferred_element_type=F32) * factor + bias
    shifted = jnp.exp(scores - jnp.max(scores, -1, keepdims=True))
    return shifted * (1.0 / jnp.sum(shifted, -1, keepdims=True))


def key_values(head, rows_v, left_v, right_v, rows_a, left_a, right_a):
    size = left_v.shape[-1] // 2
    keys, values = [], []
    for left, rows, right in ((left_v, rows_v, right_v), (left_a, rows_a, right_a)):
        keys += [left[head, :, :size], rows[head, :, size : 2 * size], right[head, :, :size]]
        values += [left[head, :, size:], rows[head, :, 2 * size :], right[head, :, size:]]
    return jnp.concatenate(keys, 0), jnp.concatenate(values, 0)


def forward_kernel(
    rows_v, left_v, right_v, rows_a, left_a, right_a, bias, w_out, heads_out, field, total, *, part
):
    step = pl.program_id(0)
    group, tokens, size = heads_out.shape
    own = (rows_v, rows_a)[part]
    outs = []
    for head in range(group):
        keys, values = key_values(head, rows_v, left_v, right_v, rows_a, left_a, right_a)
        prob = soft(own[head, :, :size], keys, bias[0], size**-0.5)
        out = jnp.dot(prob.astype(BF16), values, preferred_element_type=F32).astype(BF16)
        heads_out[head] = out
        outs.append(out)
    term = jnp.dot(
        jnp.concatenate(outs, 1),
        w_out[...].reshape(group * size, w_out.shape[-1]),
        preferred_element_type=F32,
    )

    @pl.when(step == 0)
    def _():
        total[...] = term

    @pl.when(step > 0)
    def _():
        total[...] += term

    @pl.when(step == pl.num_programs(0) - 1)
    def _():
        field[...] = total[...].astype(BF16)


def head_block(group, array):
    return pl.BlockSpec((group,) + array.shape[1:], lambda i: (i, 0, 0))


def attend(keys, bias, w_out, part):
    heads, size, width = w_out.shape
    tokens = keys[0].shape[1]
    group = 2 if heads % 2 == 0 else 1
    flops = 2 * heads * tokens * size * (12 * tokens + width)
    return pl.pallas_call(
        functools.partial(forward_kernel, part=part),
        grid=(heads // group,),
        out_shape=(
            jax.ShapeDtypeStruct((heads, tokens, size), BF16),
            jax.ShapeDtypeStruct((tokens, width), BF16),
        ),
        in_specs=[head_block(group, array) for array in keys]
        + [
            pl.BlockSpec((1,) + bias.shape[1:], lambda i: (part, 0, 0)),
            head_block(group, w_out),
        ],
        out_specs=(
            pl.BlockSpec((group, tokens, size), lambda i: (i, 0, 0)),
            pl.BlockSpec((tokens, width), lambda i: (0, 0)),
        ),
        scratch_shapes=[pltpu.VMEM((tokens, width), F32)],
        compiler_params=pltpu.CompilerParams(vmem_limit_bytes=24 * 2**20),
        cost_estimate=pl.CostEstimate(
            flops=flops, bytes_accessed=heads * size * width * 2, transcendentals=0
        ),
        name="attend",
    )(*keys, bias, w_out)


def backward_kernel(
    rows_v,
    left_v,
    right_v,
    rows_a,
    left_a,
    right_a,
    bias,
    grad_v,
    grad_a,
    w_out_v,
    w_out_a,
    own_v,
    own_a,
    to_left,
    to_right,
):
    group, tokens, triple = rows_v.shape
    size = triple // 3
    factor = size**-0.5
    both_bias = bias[...].reshape(2 * tokens, 6 * tokens)
    width = w_out_v.shape[-1]
    grads_out = [
        lax.dot_general(
            grad[...], w_out[...].reshape(group * size, width), NT, preferred_element_type=F32
        ).astype(BF16)
        for grad, w_out in ((grad_v, w_out_v), (grad_a, w_out_a))
    ]
    for head in range(group):
        keys, values = key_values(head, rows_v, left_v, right_v, rows_a, left_a, right_a)
        queries = jnp.concatenate([rows_v[head, :, :size], rows_a[head, :, :size]], 0)
        grad_out = jnp.concatenate([g[:, head * size : (head + 1) * size] for g in grads_out], 0)
        prob = soft(queries, keys, both_bias, factor)
        grad_prob = lax.dot_general(grad_out, values, NT, preferred_element_type=F32)
        center = jnp.sum(prob * grad_prob, -1, keepdims=True)
        dscore = (prob * (grad_prob - center) * factor).astype(BF16)
        dquery = jnp.dot(dscore, keys, preferred_element_type=F32)
        dkey = lax.dot_general(dscore, queries, TN, preferred_element_type=F32)
        dvalue = lax.dot_general(prob.astype(BF16), grad_out, TN, preferred_element_type=F32)
        for part, own in enumerate((own_v, own_a)):
            base = 3 * tokens * part
            middle = slice(base + tokens, base + 2 * tokens)
            own[head, :, :size] = dquery[part * tokens : (part + 1) * tokens]
            own[head, :, size : 2 * size] = dkey[middle]
            own[head, :, 2 * size :] = dvalue[middle]
            for target, start in ((to_left, base), (to_right, base + 2 * tokens)):
                target[part, head, :, :size] = dkey[start : start + tokens].astype(BF16)
                target[part, head, :, size:] = dvalue[start : start + tokens].astype(BF16)


def attend_back(keys, bias, grad_v, grad_a, w_out_v, w_out_a):
    heads, size, width = w_out_v.shape
    tokens = keys[0].shape[1]
    group = 2 if heads % 2 == 0 else 1
    whole = pl.BlockSpec((tokens, width), lambda i: (0, 0))
    own = jax.ShapeDtypeStruct((heads, tokens, 3 * size), F32)
    sent = jax.ShapeDtypeStruct((2, heads, tokens, 2 * size), BF16)
    sent_block = pl.BlockSpec((2, group, tokens, 2 * size), lambda i: (0, i, 0, 0))
    flops = 4 * heads * tokens * size * (30 * tokens + width)
    return pl.pallas_call(
        backward_kernel,
        grid=(heads // group,),
        out_shape=(own, own, sent, sent),
        in_specs=[head_block(group, array) for array in keys]
        + [
            pl.BlockSpec(bias.shape, lambda i: (0, 0, 0)),
            whole,
            whole,
            head_block(group, w_out_v),
            head_block(group, w_out_a),
        ],
        out_specs=(head_block(group, own), head_block(group, own), sent_block, sent_block),
        compiler_params=pltpu.CompilerParams(vmem_limit_bytes=40 * 2**20),
        cost_estimate=pl.CostEstimate(
            flops=flops, bytes_accessed=2 * heads * size * width * 2, transcendentals=0
        ),
        name="attend_back",
    )(*keys, bias, grad_v, grad_a, w_out_v, w_out_a)


def project(normed, weight):
    return jnp.einsum("nd,dhe->hne", normed, weight, preferred_element_type=F32).astype(BF16)


def inverse_rms(current):
    return lax.rsqrt(jnp.mean(current * current, -1, keepdims=True) + EPSILON)


def norm_back(current, inv_rms, modulation, grad_normed):
    scaled = grad_normed * modulation
    return inv_rms * scaled - current * inv_rms**3 * jnp.mean(scaled * current, -1, keepdims=True)


def local(
    video_tokens,
    audio_tokens,
    qkv_video,
    out_video,
    qkv_audio,
    out_audio,
    gain_video,
    gain_audio,
    time_from,
    time_to,
    time_steps,
    windows,
    intersection,
):
    tokens = video_tokens.shape[1]
    size = out_video.shape[1]
    bias, mods = prepare(
        time_steps, windows, intersection, time_from, time_to, gain_video, gain_audio, tokens
    )

    def normalise(current, inv_rms, row):
        return (current * inv_rms * mods[row : row + 1]).astype(BF16)

    def widen(normed_v, normed_a):
        keys = []
        for normed, weight in ((normed_v, qkv_video), (normed_a, qkv_audio)):
            rows = project(normed, weight)
            sent = rows[:, :, size:]
            keys += [rows, shift(sent, "vid", 1), shift(sent, "vid", -1)]
        return keys

    def network(normed_v, normed_a):
        keys = widen(normed_v, normed_a)
        heads_v, field_v = attend(keys, bias, out_video, 0)
        sum_v = sum_groups(field_v)
        heads_a, field_a = attend(keys, bias, out_audio, 1)
        sum_a = sum_groups(field_a)
        return sum_v, sum_a, heads_v, heads_a, keys

    start_v = video_tokens[0].astype(F32)
    start_a = audio_tokens[0].astype(F32)
    inv_v, inv_a = inverse_rms(start_v), inverse_rms(start_a)
    stride = time_steps[0, 1].astype(F32)
    euler_step = -stride / TGRID
    now_v, now_a = start_v, start_a
    for step in range(STEPS):
        field_v, field_a, *_ = network(
            normalise(now_v, inv_v if step == 0 else inverse_rms(now_v), 2 * step),
            normalise(now_a, inv_a if step == 0 else inverse_rms(now_a), 2 * step + 1),
        )
        now_v = now_v + euler_step * field_v
        now_a = now_a + euler_step * field_a
    normed_v = normalise(start_v, inv_v, 2 * STEPS)
    normed_a = normalise(start_a, inv_a, 2 * STEPS + 1)
    field_v, field_a, heads_v, heads_a, keys = network(normed_v, normed_a)

    norm_parts = scatter_columns(jnp.stack([normed_v, normed_a]))
    head_parts = gather_tokens(jnp.stack([heads_v, heads_a]))

    span = -(STEPS * stride) / TGRID
    diff_v = start_v + span * field_v - now_v
    diff_a = start_a + span * field_a - now_a
    grad_v = (span * diff_v).astype(BF16)
    grad_a = (span * diff_a).astype(BF16)
    own_v, own_a, to_left, to_right = attend_back(keys, bias, grad_v, grad_a, out_video, out_audio)
    grad_parts = scatter_columns(jnp.stack([grad_v, grad_a]))
    returned = shift(to_left, "vid", -1).astype(F32) + shift(to_right, "vid", 1).astype(F32)
    results = []
    for part, (own, weight, start, inv, row, diff) in enumerate(
        (
            (own_v, qkv_video, start_v, inv_v, 2 * STEPS, diff_v),
            (own_a, qkv_audio, start_a, inv_a, 2 * STEPS + 1, diff_a),
        )
    ):
        dqkv = jnp.concatenate(
            [own[:, :, :size], own[:, :, size:] + returned[part]], -1
        ).astype(BF16)
        dqkv_parts = gather_tokens(dqkv)
        back = sum_groups(
            jnp.einsum("hne,dhe->nd", dqkv, weight, preferred_element_type=F32).astype(BF16)
        )
        d_tokens = (diff + norm_back(start, inv, mods[row : row + 1], back)).astype(BF16)
        w_qkv = reduce_late(
            jnp.einsum(
                "slnd,shne->ldhe", norm_parts[:, :, part], dqkv_parts, preferred_element_type=F32
            )
        )
        w_out = reduce_late(
            jnp.einsum(
                "shne,slnf->lhef",
                head_parts[:, part],
                grad_parts[:, :, part],
                preferred_element_type=F32,
            )
        )
        results.append((d_tokens[None], w_qkv, w_out))
    (d_video, wqkv_v, wout_v), (d_audio, wqkv_a, wout_a) = results
    return (d_video, d_audio, wqkv_v, wout_v, wqkv_a, wout_a)


def solution(mesh):
    return jax.shard_map(
        local,
        mesh=mesh,
        in_specs=(
            P("clip", "vid", None),
            P("clip", "vid", None),
            P(None, "aud", None),
            P("aud", None, None),
            P(None, "aud", None),
            P("aud", None, None),
            P(),
            P(),
            P(),
            P(),
            P("clip", None),
            P("clip", None),
            P("clip", None, None),
        ),
        out_specs=(
            P("clip", "vid", None),
            P("clip", "vid", None),
            P(("clip", "vid"), "aud", None),
            P("aud", None, ("clip", "vid")),
            P(("clip", "vid"), "aud", None),
            P("aud", None, ("clip", "vid")),
        ),
        check_vma=False,
    )
```

time: 940 us -> 420 us (0.45)
  waiting for transfers between devices: 509 us -> 147 us
  matrix products: 196 us -> 64.1 us
  local copies, waits for them, and re-layouts: 85.4 us -> 27.3 us
  other arithmetic: 98.9 us -> 44.9 us
  starting transfers between devices: 23.6 us -> 75.8 us
  Pallas kernels: 0 us -> 50.5 us
  between operations: 18.6 us -> 2.69 us
    reduce_scatter x2 -> x0, waiting for transfers between devices: 272 us -> none  [the longest x1 136 us: local(): lax.psum_scatter(audio_wqkv.astype(jnp.bfloat16), ('clip', 'vid'), scatte...]
    ppermute x8 -> x41, waiting for transfers between devices: 0.02 us -> 147 us  [the longest x19 122 us: swap(): return lax.ppermute(block, axis, [(i, i ^ 1 << bit) for i in range(count)])]
    unnamed x9 -> x0, waiting for transfers between devices: 134 us -> none
    dot_general x41 -> x12, matrix products: 196 us -> 64.1 us  [the longest x6 42.3 us: project(): jnp.einsum('nd,dhe->hne', normed, weight, preferred_element_type=F32)]
    psum x3 -> x0, waiting for transfers between devices: 104 us -> none  [the longest x1 69.1 us: network(): lax.psum(video_part.astype(jnp.bfloat16), 'aud').astype(jnp.float32)]
    ppermute x8 -> x41, starting transfers between devices: 22.4 us -> 75.8 us  [the longest x14 38.1 us: shift(): return lax.ppermute(block, axis, route)]
    pallas_call x0 -> x8, Pallas kernels: none -> 50.5 us  [the longest x6 35.4 us: attend(): pl.pallas_call(functools.partial(forward_kernel, part=part), grid=(heads...]
    gather x15 -> x0, other arithmetic: 40.2 us -> none  [the longest x11 10.4 us: local(): low_block[key_blk][None, :]]
  transfers between devices with their start and end apart: 15 -> 41, of which waited for: 6 -> 12; matrix products, arithmetic and copies ran while one was open for 19% -> 28% of each run, Pallas kernels for 0% -> 12%
where the time goes in v1:
time: 420 us; the launch traced here: 413 us
  waiting for transfers between devices  147 us (35%)
  starting transfers between devices  75.8 us (18%)
  matrix products  64.1 us (15%)
  Pallas kernels  50.5 us (12%)
  other arithmetic  44.9 us (11%)
  local copies, waits for them, and re-layouts  27.3 us (6%)
    ppermute x19, waiting for transfers between devices, swap(): return lax.ppermute(block, axis, [(i, i ^ 1 << bit) for i in range(count)])  122 us
    dot_general x6, matrix products, project(): jnp.einsum('nd,dhe->hne', normed, weight, preferred_element_type=F32)  42.3 us
    ppermute x14, starting transfers between devices, shift(): return lax.ppermute(block, axis, route)  38.1 us
    pallas_call x6, Pallas kernels, attend(): pl.pallas_call(functools.partial(forward_kernel, part=part), grid=(heads...  35.4 us
    ppermute x19, starting transfers between devices, swap(): return lax.ppermute(block, axis, [(i, i ^ 1 << bit) for i in range(count)])  30.4 us
    ppermute x8, waiting for transfers between devices, sum_groups(): lax.ppermute(partial, 'aud', [(i, i ^ step) for i in range(count)])  24.9 us
    dot_general x2, matrix products, local(): jnp.einsum('hne,dhe->nd', dqkv, weight, preferred_element_type=F32)  14 us
    pallas_call x1, Pallas kernels, attend_back(): pl.pallas_call(backward_kernel, grid=(heads // group,), out_shape=(own, o...  12.8 us
  transfers between devices with their start and end apart: 41, of which 12 were waited for; matrix products, arithmetic and copies ran while one was open for 28% of the time, Pallas kernels for 12%

profile of v1, /device:TPU:0, one launch (start us, length us, event | category | flops | bytes accessed | tf_op | source)
XLA Modules:
  0.0 412.6 jit_solution(16284888385920990053)
XLA Ops:
  7.5 7.7 %fusion.94.rows_v = bf16[8,128,384]{2,1,0:T(8,128)(2,1)S(1)} fusion(bf16[2048,8,384]{2,1,0:T(8,128)(2,1)} %param.15, bf16[1,128,2048]{2,1,0:T(8,128)(2,1)} %param.13, f32[2048]{0:T(1024)S(1)} %bitcast.341, f32[128]{0:T(128)S(1)} %get-tuple-element.81), kind=kOutput, calls=%fused_computation.77 | convolution fusion | flops 1612054528 | bytes 13902336 | tf_op jit(solution)/shard_map/nd,dhe->hne/dot_general | solution.py:323
  24.0 5.2 %collective-permute-start.7 = (bf16[8,128,256]{2,1,0:T(8,128)(2,1)S(1)}, bf16[8,128,256]{2,1,0:T(8,128)(2,1)S(1)}, u32[]{:S(2)}, u32[]{:S(2)}) collective-permute-start(bf16[8,128,256]{2,1,0:T(8,128)(2,1)S(1)} %slice.105), channel_id=1, source_target_pairs={{0,2},{2,4},{4,6},{1,3},{3,5},{5,7},{8,10},{10,12},{12,14},{9,11},... | collective-permute-start | bytes 1572872 | tf_op jit(solution)/shard_map/ppermute | solution.py:29
  30.5 7.5 %fusion.97.rows_v = bf16[8,128,384]{2,1,0:T(8,128)(2,1)S(1)} fusion(bf16[2048,8,384]{2,1,0:T(8,128)(2,1)} %param.15, bf16[1,128,2048]{2,1,0:T(8,128)(2,1)S(1)} %copy-done.5, f32[2048]{0:T(1024)S(1)} %bitcast.332, f32[128]{0:T(128)S(1)} %get-tuple-element.81), kind=kOutput, calls=%fused_computation.78 | convolution fusion | flops 1612054528 | bytes 13902336 | tf_op jit(solution)/shard_map/nd,dhe->hne/dot_general | solution.py:323
  44.1 6.1 %attend.7 = (bf16[8,128,128]{2,1,0:T(8,128)(2,1)}, bf16[128,2048]{1,0:T(8,128)(2,1)S(1)}) custom-call(bf16[8,128,384]{2,1,0:T(8,128)(2,1)S(1)} %fusion.94.rows_v, bf16[8,128,256]{2,1,0:T(8,128)(2,1)S(1)} %collective-permute-done.5.left_v, bf16[8,128,256]{2,1,0:T(8,128)(2,1)S(1)} %collective-permute-done.6.right_v, bf16[8,128,384]{2,1,0:T(8,128)(2,1)S(1)} %fusion.85.rows_a, ...), custom_call_target="tpu_custom_call" | custom-call | flops 939524096 | bytes 4194304 | tf_op jit(solution)/shard_map/attend/pallas_call | solution.py:217
  51.8 7.5 %fusion.88.rows_a = bf16[8,128,384]{2,1,0:T(8,128)(2,1)S(1)} fusion(bf16[2048,8,384]{2,1,0:T(8,128)(2,1)} %param.17, bf16[1,128,2048]{2,1,0:T(8,128)(2,1)S(1)} %copy-done.6, f32[2048]{0:T(1024)S(1)} %bitcast.328, f32[128]{0:T(128)S(1)} %get-tuple-element.79), kind=kOutput, calls=%fused_computation.75 | convolution fusion | flops 1612054528 | bytes 13902336 | tf_op jit(solution)/shard_map/nd,dhe->hne/dot_general | solution.py:323
  65.9 6.1 %attend.8 = (bf16[8,128,128]{2,1,0:T(8,128)(2,1)}, bf16[128,2048]{1,0:T(8,128)(2,1)S(1)}) custom-call(bf16[8,128,384]{2,1,0:T(8,128)(2,1)S(1)} %fusion.94.rows_v, bf16[8,128,256]{2,1,0:T(8,128)(2,1)S(1)} %collective-permute-done.5.left_v, bf16[8,128,256]{2,1,0:T(8,128)(2,1)S(1)} %collective-permute-done.6.right_v, bf16[8,128,384]{2,1,0:T(8,128)(2,1)S(1)} %fusion.85.rows_a, ...), custom_call_target="tpu_custom_call" | custom-call | flops 939524096 | bytes 4194304 | tf_op jit(solution)/shard_map/attend/pallas_call | solution.py:217
  72.9 7.4 %fusion.91.rows_v = bf16[8,128,384]{2,1,0:T(8,128)(2,1)S(1)} fusion(bf16[2048,8,384]{2,1,0:T(8,128)(2,1)} %param.15, f32[2048]{0:T(1024)S(1)} %bitcast.337, f32[128]{0:T(128)S(1)} %add_rsqrt_fusion.1, bf16[1,128,2048]{2,1,0:T(8,128)(2,1)S(1)} %copy-done.5, bf16[128,2048]{1,0:T(8,128)(2,1)S(1)} %collective-permute-done.9, ...), kind=kOutput, calls=%fused_computation.76 | convolution fusion | flops 1613365248 | bytes 14950916 | tf_op jit(solution)/shard_map/nd,dhe->hne/dot_general | solution.py:323
  88.9 7.4 %fusion.82.rows_a = bf16[8,128,384]{2,1,0:T(8,128)(2,1)S(1)} fusion(bf16[2048,8,384]{2,1,0:T(8,128)(2,1)} %param.17, f32[2048]{0:T(1024)S(1)} %bitcast.336, f32[128]{0:T(128)S(1)} %add_rsqrt_fusion, bf16[1,128,2048]{2,1,0:T(8,128)(2,1)S(1)} %copy-done.6, bf16[128,2048]{1,0:T(8,128)(2,1)S(1)} %collective-permute-done.12, ...), kind=kOutput, calls=%fused_computation.73 | convolution fusion | flops 1613365248 | bytes 14950916 | tf_op jit(solution)/shard_map/nd,dhe->hne/dot_general | solution.py:323
  104.1 5.5 %attend.6 = (bf16[8,128,128]{2,1,0:T(8,128)(2,1)S(1)}, bf16[128,2048]{1,0:T(8,128)(2,1)S(1)}) custom-call(bf16[8,128,384]{2,1,0:T(8,128)(2,1)S(1)} %fusion.97.rows_v, bf16[8,128,256]{2,1,0:T(8,128)(2,1)S(1)} %collective-permute-done.left_v, bf16[8,128,256]{2,1,0:T(8,128)(2,1)S(1)} %collective-permute-done.1.right_v, bf16[8,128,384]{2,1,0:T(8,128)(2,1)S(1)} %fusion.88.rows_a, ...), custom_call_target="tpu_custom_call" | custom-call | flops 939524096 | bytes 4194304 | tf_op jit(solution)/shard_map/attend/pallas_call | solution.py:217
  110.2 6.1 %attend.9 = (bf16[8,128,128]{2,1,0:T(8,128)(2,1)}, bf16[128,2048]{1,0:T(8,128)(2,1)S(1)}) custom-call(bf16[8,128,384]{2,1,0:T(8,128)(2,1)S(1)} %fusion.91.rows_v, bf16[8,128,256]{2,1,0:T(8,128)(2,1)S(1)} %collective-permute-done.10.left_v, bf16[8,128,256]{2,1,0:T(8,128)(2,1)S(1)} %collective-permute-done.11.right_v, bf16[8,128,384]{2,1,0:T(8,128)(2,1)S(1)} %fusion.82.rows_a, ...), custom_call_target="tpu_custom_call" | custom-call | flops 939524096 | bytes 4194304 | tf_op jit(solution)/shard_map/attend/pallas_call | solution.py:217
  118.9 5.5 %attend.10 = (bf16[8,128,128]{2,1,0:T(8,128)(2,1)S(1)}, bf16[128,2048]{1,0:T(8,128)(2,1)S(1)}) custom-call(bf16[8,128,384]{2,1,0:T(8,128)(2,1)S(1)} %fusion.97.rows_v, bf16[8,128,256]{2,1,0:T(8,128)(2,1)S(1)} %collective-permute-done.left_v, bf16[8,128,256]{2,1,0:T(8,128)(2,1)S(1)} %collective-permute-done.1.right_v, ...), custom_call_target="tpu_custom_call" | custom-call | flops 939524096 | bytes 4194304 | tf_op jit(solution)/shard_map/attend/pallas_call | solution.py:217
  127.4 6.1 %attend.11 = (bf16[8,128,128]{2,1,0:T(8,128)(2,1)}, bf16[128,2048]{1,0:T(8,128)(2,1)S(1)}) custom-call(bf16[8,128,384]{2,1,0:T(8,128)(2,1)S(1)} %fusion.91.rows_v, bf16[8,128,256]{2,1,0:T(8,128)(2,1)S(1)} %collective-permute-done.10.left_v, bf16[8,128,256]{2,1,0:T(8,128)(2,1)S(1)} %collective-permute-done.11.right_v, ...), custom_call_target="tpu_custom_call" | custom-call | flops 939524096 | bytes 4194304 | tf_op jit(solution)/shard_map/attend/pallas_call | solution.py:217
  136.6 8.9 %collective-permute-done.16 = bf16[128,2048]{1,0:T(8,128)(2,1)S(1)} collective-permute-done((bf16[128,2048]{1,0:T(8,128)(2,1)S(1)}, bf16[128,2048]{1,0:T(8,128)(2,1)S(1)}, u32[]{:S(2)}, u32[]{:S(2)}) %collective-permute-start.16) | collective-permute-done | bytes 524320 | tf_op jit(solution)/shard_map/ppermute | solution.py:81
  145.5 11.2 %collective-permute-done.17 = bf16[128,2048]{1,0:T(8,128)(2,1)S(1)} collective-permute-done((bf16[128,2048]{1,0:T(8,128)(2,1)S(1)}, bf16[128,2048]{1,0:T(8,128)(2,1)S(1)}, u32[]{:S(2)}, u32[]{:S(2)}) %collective-permute-start.17) | collective-permute-done | bytes 524320 | tf_op jit(solution)/shard_map/ppermute | solution.py:81
  158.5 12.8 %attend_back.1 = (f32[8,128,384]{2,1,0:T(8,128)S(1)}, f32[8,128,384]{2,1,0:T(8,128)S(1)}, bf16[2,8,128,256]{3,2,1,0:T(8,128)(2,1)}, bf16[2,8,128,256]{3,2,1,0:T(8,128)(2,1)}) custom-call(bf16[8,128,384]{2,1,0:T(8,128)(2,1)S(1)} %fusion.97.rows_v, bf16[8,128,256]{2,1,0:T(8,128)(2,1)S(1)} %collective-permute-done.left_v, ...), custom_call_target="tpu_custom_call" | custom-call | flops 3087007744 | bytes 8388608 | tf_op jit(solution)/shard_map/attend_back/pallas_call | solution.py:301
  197.9 8.9 %collective-permute-start.23 = (bf16[2,2,2,2,128,128]{5,4,3,2,1,0:T(8,128)(2,1)}, bf16[2,2,2,2,128,128]{5,4,3,2,1,0:T(8,128)(2,1)}, u32[]{:S(2)}, u32[]{:S(2)}) collective-permute-start(bf16[2,2,2,2,128,128]{5,4,3,2,1,0:T(8,128)(2,1)} %get-tuple-element.68), channel_id=1, source_target_pairs={{0,4},{2,6},{4,0},{6,2},{1,5},{3,7},{5,1},{7,3},{8,12},{10,14},{12... | collective-permute-start | bytes 1572872 | tf_op jit(solution)/shard_map/ppermute | solution.py:23
  208.3 14.0 %collective-permute-done.33 = bf16[2,2,8,128,128]{4,3,2,1,0:T(8,128)(2,1)S(1)} collective-permute-done((bf16[2,2,8,128,128]{4,3,2,1,0:T(8,128)(2,1)S(1)}, bf16[2,2,8,128,128]{4,3,2,1,0:T(8,128)(2,1)S(1)}, u32[]{:S(2)}, u32[]{:S(2)}) %collective-permute-start.33) | collective-permute-done | bytes 1048608 | tf_op jit(solution)/shard_map/ppermute | solution.py:23
  233.9 5.1 %fusion.31 = bf16[128,2048]{1,0:T(8,128)(2,1)} fusion(bf16[2048,8,384]{2,1,0:T(8,128)(2,1)S(1)} %bitcast.309, bf16[8,128,256]{2,1,0:T(8,128)(2,1)S(1)} %get-tuple-element.59, bf16[8,128,128]{2,1,0:T(8,128)(2,1)S(1)} %copy-done.33), kind=kOutput, calls=%fused_computation.30 | convolution fusion | flops 1612447744 | bytes 13893632 | tf_op jit(solution)/shard_map/hne,dhe->nd/dot_general | solution.py:415
  244.9 8.9 %fusion.28 = bf16[128,2048]{1,0:T(8,128)(2,1)S(1)} fusion(bf16[2048,8,384]{2,1,0:T(8,128)(2,1)} %param.17, bf16[8,128,256]{2,1,0:T(8,128)(2,1)S(1)} %get-tuple-element.58, bf16[8,128,128]{2,1,0:T(8,128)(2,1)S(1)} %copy-done.32), kind=kOutput, calls=%fused_computation.29 | convolution fusion | flops 1612447744 | bytes 13893632 | tf_op jit(solution)/shard_map/hne,dhe->nd/dot_general | solution.py:415
  265.4 13.2 %collective-permute-done.26 = bf16[2,8,128,384]{3,2,1,0:T(8,128)(2,1)} collective-permute-done((bf16[2,8,128,384]{3,2,1,0:T(8,128)(2,1)}, bf16[2,8,128,384]{3,2,1,0:T(8,128)(2,1)}, u32[]{:S(2)}, u32[]{:S(2)}) %collective-permute-start.26) | collective-permute-done | bytes 1572896 | tf_op jit(solution)/shard_map/ppermute | solution.py:23
  284.2 22.4 %collective-permute-done.37 = bf16[2,8,128,384]{3,2,1,0:T(8,128)(2,1)} collective-permute-done((bf16[2,8,128,384]{3,2,1,0:T(8,128)(2,1)}, bf16[2,8,128,384]{3,2,1,0:T(8,128)(2,1)}, u32[]{:S(2)}, u32[]{:S(2)}) %collective-permute-start.37) | collective-permute-done | bytes 1572896 | tf_op jit(solution)/shard_map/ppermute | solution.py:23
  333.5 36.3 %collective-permute-done.35 = bf16[1,8,128,128]{2,3,1,0:T(8,128)(2,1)S(1)} collective-permute-done((bf16[1,8,128,128]{2,3,1,0:T(8,128)(2,1)S(1)}, bf16[1,8,128,128]{2,3,1,0:T(8,128)(2,1)S(1)}, u32[]{:S(2)}, u32[]{:S(2)}) %collective-permute-start.35) | collective-permute-done | bytes 262176 | tf_op jit(solution)/shard_map/ppermute | solution.py:23
  377.7 14.7 %collective-permute-done.28 = bf16[1,128,8,384]{3,1,2,0:T(8,128)(2,1)} collective-permute-done((bf16[1,128,8,384]{3,1,2,0:T(8,128)(2,1)S(1)}, bf16[1,128,8,384]{3,1,2,0:T(8,128)(2,1)}, u32[]{:S(2)}, u32[]{:S(2)}) %collective-permute-start.28) | collective-permute-done | bytes 786464 | tf_op jit(solution)/shard_map/ppermute | solution.py:23
  396.2 12.5 %collective-permute-done.39 = bf16[1,128,8,384]{3,1,2,0:T(8,128)(2,1)} collective-permute-done((bf16[1,128,8,384]{3,1,2,0:T(8,128)(2,1)S(1)}, bf16[1,128,8,384]{3,1,2,0:T(8,128)(2,1)}, u32[]{:S(2)}, u32[]{:S(2)}) %collective-permute-start.39) | collective-permute-done | bytes 786464 | tf_op jit(solution)/shard_map/ppermute | solution.py:23
  (227 shorter events, 162.8 us)
Async XLA Ops:
  15.3 27.0 %collective-permute-start.5 = (bf16[8,128,256]{2,1,0:T(8,128)(2,1)S(1)}, bf16[8,128,256]{2,1,0:T(8,128)(2,1)S(1)}, u32[]{:S(2)}, u32[]{:S(2)}) collective-permute-start(bf16[8,128,256]{2,1,0:T(8,128)(2,1)S(1)} %slice.104), channel_id=1, source_target_pairs={{0,2},{2,4},{4,6},{1,3},{3,5},{5,7},{8,10},{10,12},{12,14},{9,11},... | collective-permute-start | bytes 1572872 | tf_op jit(solution)/shard_map/ppermute | solution.py:29
  17.7 26.4 %collective-permute-start.6 = (bf16[8,128,256]{2,1,0:T(8,128)(2,1)S(1)}, bf16[8,128,256]{2,1,0:T(8,128)(2,1)S(1)}, u32[]{:S(2)}, u32[]{:S(2)}) collective-permute-start(bf16[8,128,256]{2,1,0:T(8,128)(2,1)S(1)} %slice.104), channel_id=1, source_target_pairs={{2,0},{4,2},{6,4},{3,1},{5,3},{7,5},{10,8},{12,10},{14,12},{11,9},... | collective-permute-start | bytes 1572872 | tf_op jit(solution)/shard_map/ppermute | solution.py:29
  38.1 58.4 %collective-permute-start = (bf16[8,128,256]{2,1,0:T(8,128)(2,1)S(1)}, bf16[8,128,256]{2,1,0:T(8,128)(2,1)S(1)}, u32[]{:S(2)}, u32[]{:S(2)}) collective-permute-start(bf16[8,128,256]{2,1,0:T(8,128)(2,1)S(1)} %slice.102), channel_id=1, source_target_pairs={{0,2},{2,4},{4,6},{1,3},{3,5},{5,7},{8,10},{10,12},{12,14},{9,11},... | collective-permute-start | bytes 1572872 | tf_op jit(solution)/shard_map/ppermute | solution.py:29
  42.3 55.4 %collective-permute-start.1 = (bf16[8,128,256]{2,1,0:T(8,128)(2,1)S(1)}, bf16[8,128,256]{2,1,0:T(8,128)(2,1)S(1)}, u32[]{:S(2)}, u32[]{:S(2)}) collective-permute-start(bf16[8,128,256]{2,1,0:T(8,128)(2,1)S(1)} %slice.102), channel_id=1, source_target_pairs={{2,0},{4,2},{6,4},{3,1},{5,3},{7,5},{10,8},{12,10},{14,12},{11,9},... | collective-permute-start | bytes 1572872 | tf_op jit(solution)/shard_map/ppermute | solution.py:29
  59.3 43.3 %collective-permute-start.2 = (bf16[8,128,256]{2,1,0:T(8,128)(2,1)S(1)}, bf16[8,128,256]{2,1,0:T(8,128)(2,1)S(1)}, u32[]{:S(2)}, u32[]{:S(2)}) collective-permute-start(bf16[8,128,256]{2,1,0:T(8,128)(2,1)S(1)} %slice.103), channel_id=1, source_target_pairs={{0,2},{2,4},{4,6},{1,3},{3,5},{5,7},{8,10},{10,12},{12,14},{9,11},... | collective-permute-start | bytes 1572872 | tf_op jit(solution)/shard_map/ppermute | solution.py:29
  63.3 40.8 %collective-permute-start.3 = (bf16[8,128,256]{2,1,0:T(8,128)(2,1)S(1)}, bf16[8,128,256]{2,1,0:T(8,128)(2,1)S(1)}, u32[]{:S(2)}, u32[]{:S(2)}) collective-permute-start(bf16[8,128,256]{2,1,0:T(8,128)(2,1)S(1)} %slice.103), channel_id=1, source_target_pairs={{2,0},{4,2},{6,4},{3,1},{5,3},{7,5},{10,8},{12,10},{14,12},{11,9},... | collective-permute-start | bytes 1572872 | tf_op jit(solution)/shard_map/ppermute | solution.py:29
  125.8 57.2 %collective-permute-start.32 = (bf16[1,2,8,128,128]{4,3,2,1,0:T(8,128)(2,1)}, bf16[1,2,8,128,128]{4,3,2,1,0:T(8,128)(2,1)}, u32[]{:S(2)}, u32[]{:S(2)}) collective-permute-start(bf16[1,2,8,128,128]{4,3,2,1,0:T(8,128)(2,1)} %maximum_bitcast_fusion), channel_id=1, source_target_pairs={{0,8},{8,0},{16,24},{24,16},{1,9},{9,1},{17,25},{25,17},{2,10},{10... | collective-permute-start | bytes 1572872 | tf_op jit(solution)/shard_map/ppermute | solution.py:23
  184.3 38.0 %collective-permute-start.33 = (bf16[2,2,8,128,128]{4,3,2,1,0:T(8,128)(2,1)S(1)}, bf16[2,2,8,128,128]{4,3,2,1,0:T(8,128)(2,1)S(1)}, u32[]{:S(2)}, u32[]{:S(2)}) collective-permute-start(bf16[2,2,8,128,128]{4,3,2,1,0:T(8,128)(2,1)S(1)} %pad_maximum_fusion.10), channel_id=1, source_target_pairs={{0,4},{2,6},{4,0},{6,2},{1,5},{3,7},{5,1},{7,3},{8,12},{10,14},{12... | collective-permute-start | bytes 3145736 | tf_op jit(solution)/shard_map/ppermute | solution.py:23
  188.5 37.0 %collective-permute-start.29 = (bf16[1,2,2,2,2,128,128]{6,5,4,3,2,1,0:T(8,128)(2,1)S(1)}, bf16[1,2,2,2,2,128,128]{6,5,4,3,2,1,0:T(8,128)(2,1)S(1)}, u32[]{:S(2)}, u32[]{:S(2)}) collective-permute-start(bf16[1,2,2,2,2,128,128]{6,5,4,3,2,1,0:T(8,128)(2,1)S(1)} %get-tuple-element.64), channel_id=1, source_target_pairs={{0,8},{8,0},{16,24},{24,16},{1,9},{9,1},{17,25},{25,17},{2,10},{10... | collective-permute-start | bytes 1572872 | tf_op jit(solution)/shard_map/ppermute | solution.py:23
  192.0 37.6 %collective-permute-start.25 = (bf16[1,8,128,384]{3,2,1,0:T(8,128)(2,1)S(1)}, bf16[1,8,128,384]{3,2,1,0:T(8,128)(2,1)S(1)}, u32[]{:S(2)}, u32[]{:S(2)}) collective-permute-start(bf16[1,8,128,384]{3,2,1,0:T(8,128)(2,1)S(1)} %pad_maximum_fusion.11), channel_id=1, source_target_pairs={{0,8},{8,0},{16,24},{24,16},{1,9},{9,1},{17,25},{25,17},{2,10},{10... | collective-permute-start | bytes 2359304 | tf_op jit(solution)/shard_map/ppermute | solution.py:23
  197.9 56.0 %collective-permute-start.23 = (bf16[2,2,2,2,128,128]{5,4,3,2,1,0:T(8,128)(2,1)}, bf16[2,2,2,2,128,128]{5,4,3,2,1,0:T(8,128)(2,1)}, u32[]{:S(2)}, u32[]{:S(2)}) collective-permute-start(bf16[2,2,2,2,128,128]{5,4,3,2,1,0:T(8,128)(2,1)} %get-tuple-element.68), channel_id=1, source_target_pairs={{0,4},{2,6},{4,0},{6,2},{1,5},{3,7},{5,1},{7,3},{8,12},{10,14},{12... | collective-permute-start | bytes 1572872 | tf_op jit(solution)/shard_map/ppermute | solution.py:23
  226.6 27.4 %collective-permute-start.30 = (bf16[2,2,2,2,128,128]{5,4,3,2,1,0:T(8,128)(2,1)}, bf16[2,2,2,2,128,128]{5,4,3,2,1,0:T(8,128)(2,1)}, u32[]{:S(2)}, u32[]{:S(2)}) collective-permute-start(bf16[2,2,2,2,128,128]{5,4,3,2,1,0:T(8,128)(2,1)} %get-tuple-element.62), channel_id=1, source_target_pairs={{0,4},{2,6},{4,0},{6,2},{1,5},{3,7},{5,1},{7,3},{8,12},{10,14},{12... | collective-permute-start | bytes 1572872 | tf_op jit(solution)/shard_map/ppermute | solution.py:23
  231.9 46.7 %collective-permute-start.26 = (bf16[2,8,128,384]{3,2,1,0:T(8,128)(2,1)}, bf16[2,8,128,384]{3,2,1,0:T(8,128)(2,1)}, u32[]{:S(2)}, u32[]{:S(2)}) collective-permute-start(bf16[2,8,128,384]{3,2,1,0:T(8,128)(2,1)} %pad_maximum_fusion.6), channel_id=1, source_target_pairs={{0,4},{2,6},{4,0},{6,2},{1,5},{3,7},{5,1},{7,3},{8,12},{10,14},{12... | collective-permute-start | bytes 4718600 | tf_op jit(solution)/shard_map/ppermute | solution.py:23
  239.0 41.5 %collective-permute-start.20 = (bf16[128,2048]{1,0:T(8,128)(2,1)}, bf16[128,2048]{1,0:T(8,128)(2,1)}, u32[]{:S(2)}, u32[]{:S(2)}) collective-permute-start(bf16[128,2048]{1,0:T(8,128)(2,1)} %fusion.31), channel_id=1, source_target_pairs={{0,1},{1,0},{2,3},{3,2},{4,5},{5,4},{6,7},{7,6},{8,9},{9,8},{10,11... | collective-permute-start | bytes 1572872 | tf_op jit(solution)/shard_map/ppermute | solution.py:81
  242.8 63.8 %collective-permute-start.37 = (bf16[2,8,128,384]{3,2,1,0:T(8,128)(2,1)}, bf16[2,8,128,384]{3,2,1,0:T(8,128)(2,1)}, u32[]{:S(2)}, u32[]{:S(2)}) collective-permute-start(bf16[2,8,128,384]{3,2,1,0:T(8,128)(2,1)} %pad_maximum_fusion.7), channel_id=1, source_target_pairs={{0,4},{2,6},{4,0},{6,2},{1,5},{3,7},{5,1},{7,3},{8,12},{10,14},{12... | collective-permute-start | bytes 4718600 | tf_op jit(solution)/shard_map/ppermute | solution.py:23
  253.9 57.1 %collective-permute-start.34 = (bf16[4,2,8,128,128]{4,3,2,1,0:T(8,128)(2,1)}, bf16[4,2,8,128,128]{4,3,2,1,0:T(8,128)(2,1)}, u32[]{:S(2)}, u32[]{:S(2)}) collective-permute-start(bf16[4,2,8,128,128]{4,3,2,1,0:T(8,128)(2,1)} %pad_maximum_fusion.5), channel_id=1, source_target_pairs={{0,2},{2,0},{4,6},{6,4},{1,3},{3,1},{5,7},{7,5},{8,10},{10,8},{12,... | collective-permute-start | bytes 6291464 | tf_op jit(solution)/shard_map/ppermute | solution.py:23
  254.0 28.6 %collective-permute-start.21 = (bf16[128,2048]{1,0:T(8,128)(2,1)S(1)}, bf16[128,2048]{1,0:T(8,128)(2,1)}, u32[]{:S(2)}, u32[]{:S(2)}) collective-permute-start(bf16[128,2048]{1,0:T(8,128)(2,1)S(1)} %fusion.28), channel_id=1, source_target_pairs={{0,1},{1,0},{2,3},{3,2},{4,5},{5,4},{6,7},{7,6},{8,9},{9,8},{10,11... | collective-permute-start | bytes 1572872 | tf_op jit(solution)/shard_map/ppermute | solution.py:81
  278.6 40.7 %collective-permute-start.24 = (bf16[4,2,2,128,128]{3,4,0,1,2:T(8,128)(2,1)}, bf16[4,2,2,128,128]{3,4,0,1,2:T(8,128)(2,1)S(1)}, u32[]{:S(2)}, u32[]{:S(2)}) collective-permute-start(bf16[4,2,2,128,128]{3,4,0,1,2:T(8,128)(2,1)} %bitcast.324), channel_id=1, source_target_pairs={{0,2},{2,0},{4,6},{6,4},{1,3},{3,1},{5,7},{7,5},{8,10},{10,8},{12,... | collective-permute-start | bytes 1572872 | tf_op jit(solution)/shard_map/ppermute | solution.py:23
  280.5 38.8 %collective-permute-start.27 = (bf16[4,8,128,384]{3,2,1,0:T(8,128)(2,1)S(1)}, bf16[4,8,128,384]{3,2,1,0:T(8,128)(2,1)S(1)}, u32[]{:S(2)}, u32[]{:S(2)}) collective-permute-start(bf16[4,8,128,384]{3,2,1,0:T(8,128)(2,1)S(1)} %pad_maximum_fusion.3), channel_id=1, source_target_pairs={{0,2},{2,0},{4,6},{6,4},{1,3},{3,1},{5,7},{7,5},{8,10},{10,8},{12,... | collective-permute-start | bytes 9437192 | tf_op jit(solution)/shard_map/ppermute | solution.py:23
  282.6 31.0 %collective-permute-start.31 = (bf16[4,2,2,128,128]{3,4,0,1,2:T(8,128)(2,1)S(1)}, bf16[4,2,2,128,128]{3,4,0,1,2:T(8,128)(2,1)S(1)}, u32[]{:S(2)}, u32[]{:S(2)}) collective-permute-start(bf16[4,2,2,128,128]{3,4,0,1,2:T(8,128)(2,1)S(1)} %bitcast.327), channel_id=1, source_target_pairs={{0,2},{2,0},{4,6},{6,4},{1,3},{3,1},{5,7},{7,5},{8,10},{10,8},{12,... | collective-permute-start | bytes 1572872 | tf_op jit(solution)/shard_map/ppermute | solution.py:23
  314.8 55.0 %collective-permute-start.35 = (bf16[1,8,128,128]{2,3,1,0:T(8,128)(2,1)S(1)}, bf16[1,8,128,128]{2,3,1,0:T(8,128)(2,1)S(1)}, u32[]{:S(2)}, u32[]{:S(2)}) collective-permute-start(bf16[1,8,128,128]{2,3,1,0:T(8,128)(2,1)S(1)} %fusion.192), channel_id=1, source_target_pairs={{0,16},{8,24},{16,0},{24,8},{1,17},{9,25},{17,1},{25,9},{2,18},{10... | collective-permute-start | bytes 786440 | tf_op jit(solution)/shard_map/ppermute | solution.py:23
  319.0 56.6 %collective-permute-start.40 = (bf16[1,8,128,128]{2,3,1,0:T(8,128)(2,1)}, bf16[1,8,128,128]{2,3,1,0:T(8,128)(2,1)}, u32[]{:S(2)}, u32[]{:S(2)}) collective-permute-start(bf16[1,8,128,128]{2,3,1,0:T(8,128)(2,1)} %fusion.193), channel_id=1, source_target_pairs={{0,16},{8,24},{16,0},{24,8},{1,17},{9,25},{17,1},{25,9},{2,18},{10... | collective-permute-start | bytes 786440 | tf_op jit(solution)/shard_map/ppermute | solution.py:23
  324.3 68.0 %collective-permute-start.28 = (bf16[1,128,8,384]{3,1,2,0:T(8,128)(2,1)S(1)}, bf16[1,128,8,384]{3,1,2,0:T(8,128)(2,1)}, u32[]{:S(2)}, u32[]{:S(2)}) collective-permute-start(bf16[1,128,8,384]{3,1,2,0:T(8,128)(2,1)S(1)} %dynamic-slice_convert_fusion.1), channel_id=1, source_target_pairs={{0,16},{8,24},{16,0},{24,8},{1,17},{9,25},{17,1},{25,9},{2,18},{10... | collective-permute-start | bytes 2359304 | tf_op jit(solution)/shard_map/ppermute | solution.py:23
  330.3 78.5 %collective-permute-start.39 = (bf16[1,128,8,384]{3,1,2,0:T(8,128)(2,1)S(1)}, bf16[1,128,8,384]{3,1,2,0:T(8,128)(2,1)}, u32[]{:S(2)}, u32[]{:S(2)}) collective-permute-start(bf16[1,128,8,384]{3,1,2,0:T(8,128)(2,1)S(1)} %dynamic-slice_convert_fusion), channel_id=1, source_target_pairs={{0,16},{8,24},{16,0},{24,8},{1,17},{9,25},{17,1},{25,9},{2,18},{10... | collective-permute-start | bytes 2359304 | tf_op jit(solution)/shard_map/ppermute | solution.py:23
  (55 other events, 738.1 us)
